TPU v7x, 512 devices: a whole 4x8x8 slice. The times are simulated.
512 devices in a mesh: dp: 64 (over y, x, core), tensor: 8 (over z).
Axes of the slice: x: 4, y: 8, z: 8, core: 2. Of those that a mesh axis runs over, the one named last changes fastest.
Arguments:
- queries: bfloat16 [98304, 4096], P('dp', 'tensor'), may hold values from -150 to 150
- key_rows: bfloat16 [98304, 1024], P('dp', 'tensor'), may hold values from -150 to 150
- values: bfloat16 [98304, 1024], P('dp', 'tensor'), may hold values from -6 to 6
- doc_lengths: int32 [64, 12], replicated, may hold values from 0 to 512, as said below
- swap_plan: int32 [64, 4], replicated, may hold values from -1 to 2, as said below
Outputs:
- attention_out: bfloat16 [98304, 4096], P(('dp', 'tensor'))
Inputs may be any that keep to these rules, and one draw needn't show every extreme that they name: `doc_lengths`: each row lists its documents in order, each a multiple of 128 tokens; no document crosses a multiple of 512 tokens; the documents fill whole blocks from the row's start, zeros follow the last one, and every row has at least one block of documents. `swap_plan`: entry [r, s] names a block of row r; the row whose index differs from r in bit log2(64) - 1 - s has -1 at section s exactly when r has.
All inputs are finite; a program needn't handle non-finite values.
Results may differ from a plain program's by a relative error of at most 0.0045.
Values may be sent and summed in bfloat16 or wider, within the bound.
A program may use at most 64 MiB of HBM per device.

v0:
```python
import math

import jax
import jax.numpy as jnp
from jax import lax
from jax.sharding import PartitionSpec as P

HEAD_DIM = 128
SECTIONS = 4
BLOCK = 512


def from_partner(value, axis, stride):
    mask = 2**stride
    pairs = [(source, source ^ mask) for source in range(lax.axis_size(axis))]
    return lax.ppermute(value, axis, pairs)


def token_ids(lengths_row, row_tokens):
    endings = jnp.cumsum(lengths_row)
    places = jnp.arange(row_tokens, dtype=jnp.int32)
    counted = jnp.sum((endings[None, :] <= places[:, None]).astype(jnp.int32), axis=1)
    return jnp.where(places < endings[-1], counted, -1)


def attend_block(query_block, key_block, value_block, block_ids):
    kv_heads = key_block.shape[1] // HEAD_DIM
    group_size = query_block.shape[1] // key_block.shape[1]
    query_four = query_block.reshape(BLOCK, kv_heads, group_size, HEAD_DIM)
    key_three = key_block.reshape(BLOCK, kv_heads, HEAD_DIM)
    value_three = value_block.reshape(BLOCK, kv_heads, HEAD_DIM)
    scores = jnp.einsum(
        "qhgd,khd->hgqk", query_four, key_three, preferred_element_type=jnp.float32
    ) * (1.0 / math.sqrt(HEAD_DIM))
    places = jnp.arange(BLOCK, dtype=jnp.int32)
    allowed = (
        (block_ids[:, None] == block_ids[None, :])
        & (block_ids[:, None] >= 0)
        & (places[None, :] <= places[:, None])
    )
    masked = jnp.where(allowed, scores, -1e30)
    highest = jnp.max(masked, axis=-1, keepdims=True)
    powers = jnp.where(allowed, jnp.exp(masked - highest), 0.0)
    totals = jnp.sum(powers, axis=-1, keepdims=True)
    live_rows = block_ids >= 0
    weights = (powers / jnp.where(live_rows[:, None], totals, 1.0)).astype(jnp.bfloat16)
    head_mix = jnp.einsum(
        "hgqk,khd->qhgd", weights, value_three, preferred_element_type=jnp.float32
    )
    return head_mix.reshape(BLOCK, query_block.shape[1]).astype(jnp.bfloat16)


def guarded(query_block, key_block, value_block, block_ids):
    return lax.cond(
        block_ids[0] >= 0,
        lambda: attend_block(query_block, key_block, value_block, block_ids),
        lambda: jnp.zeros((BLOCK, query_block.shape[1]), jnp.bfloat16),
    )


def local(queries, key_rows, values, doc_lengths, swap_plan):
    row_tokens = queries.shape[0]
    blocks = row_tokens // BLOCK
    query_width = queries.shape[1]
    levels = lax.axis_size("dp").bit_length() - 1
    own_rank = lax.axis_index("dp")
    own_ids = token_ids(
        lax.dynamic_index_in_dim(doc_lengths, own_rank, 0, keepdims=False), row_tokens
    )
    results = []
    for block_index in range(blocks):
        lower = block_index * BLOCK
        upper = lower + BLOCK
        results.append(
            guarded(
                queries[lower:upper],
                key_rows[lower:upper],
                values[lower:upper],
                own_ids[lower:upper],
            )
        )
    stacked = jnp.stack(results, axis=0)
    for section_index in range(SECTIONS):
        bit_number = levels - 1 - section_index
        chosen = lax.dynamic_index_in_dim(swap_plan[:, section_index], own_rank, 0, keepdims=False)
        safe_index = jnp.maximum(chosen, 0)
        outgoing = lax.dynamic_index_in_dim(stacked, safe_index, 0, keepdims=False)
        incoming = from_partner(outgoing, "dp", bit_number)
        stacked = lax.dynamic_update_index_in_dim(
            stacked, jnp.where(chosen >= 0, incoming, outgoing), safe_index, 0
        )
    attended = stacked.reshape(row_tokens, query_width)
    return lax.all_to_all(attended, "tensor", split_axis=0, concat_axis=1, tiled=True)


def solution(mesh):
    return jax.shard_map(
        local,
        mesh=mesh,
        in_specs=(P("dp", "tensor"), P("dp", "tensor"), P("dp", "tensor"), P(), P()),
        out_specs=P(("dp", "tensor"), None),
        check_vma=False,
    )
```

profile of v0, /device:TPU:42, one launch (start us, length us, event | category | flops | bytes accessed | tf_op | source)
XLA Modules:
  0.0 172.8 jit_solution(6509442166270571603)
XLA Ops:
  0.0 0.0 copy-start
  0.0 0.7 copy-done
  0.7 0.2 dynamic-slice_reduce_fusion
  0.9 0.2 reduce-window.4
  1.1 0.6 slice.76
  1.7 0.8 fusion.47
  2.5 0.1 convert_reduce_fusion
  2.6 0.7 fusion.45
  3.2 0.6 fusion.46
  5.8 7.9 %conditional.3 = (bf16[1,512,512]{2,1,0:T(8,128)(2,1)S(1)}) conditional(s32[]{:T(128)} %bitcast.32, () %tuple.29, (s32[1536]{0:T(1024)S(1)}, bf16[1536,128]{1,0:T(8,128)(2,1)}, bf16[1536,512]{1,0:T(8,128)(2,1)}, bf16[1536,128]{1,0:T(8,128)(2,1)}) %tuple.33), branch_computations={%region_2.3_spmd, %region_3.6_spmd} | conditional | flops 552860160 | bytes 21038600 | solution.py:54
  5.8 0.2 fusion.8
  6.0 1.2 copy.50
  7.2 1.7 copy.49
  9.0 1.8 %fusion = (f32[4,512]{1,0:T(4,128)S(1)}, f32[512,512,4]{1,0,2:T(8,128)S(1)}) fusion(pred[512,512]{0,1:T(8,128)(4,1)S(1)} %fusion.8, bf16[512,4,128]{0,2,1:T(8,128)(2,1)S(1)} %bitcast.153, bf16[1536,128]{1,0:T(8,128)(2,1)} %get-tuple-element.54), kind=kOutput, calls=%fused_computation.3 | convolution fusion | flops 271579136 | bytes 5120000 | tf_op jit(solution)/shard_map/cond/branch_1_fun/qhgd,khd->hgqk/dot_general | solution.py:32
  10.7 1.0 fusion.1
  11.8 1.6 fusion.5
  13.4 0.2 copy.66
  13.7 0.7 fusion.48
  14.4 0.8 conditional.5
  14.4 0.8 stack.16.clone
  15.2 10.3 %conditional.4 = (bf16[1,512,512]{2,1,0:T(8,128)(2,1)}) conditional(s32[]{:T(128)} %bitcast.33, () %tuple.31, (s32[1536]{0:T(1024)S(1)}, bf16[1536,128]{1,0:T(8,128)(2,1)}, bf16[1536,512]{1,0:T(8,128)(2,1)}, bf16[1536,128]{1,0:T(8,128)(2,1)}) %tuple.33), branch_computations={%region_6.7_spmd, %region_7.10_spmd} | conditional | flops 552860160 | bytes 21038600 | solution.py:54
  15.2 0.2 fusion.23
  15.5 1.9 %copy.52 = bf16[1536,128]{0,1:T(8,128)(2,1)} copy(bf16[1536,128]{1,0:T(8,128)(2,1)} %get-tuple-element.108) | data formatting | bytes 786432 | tf_op jit(solution)/shard_map
  17.4 1.7 copy.51
  19.1 1.8 %fusion.15 = (f32[4,512]{1,0:T(4,128)S(1)}, f32[512,512,4]{1,0,2:T(8,128)S(1)}) fusion(pred[512,512]{0,1:T(8,128)(4,1)S(1)} %fusion.23, bf16[512,4,128]{0,2,1:T(8,128)(2,1)S(1)} %bitcast.155, bf16[1536,128]{1,0:T(8,128)(2,1)} %get-tuple-element.58), kind=kOutput, calls=%fused_computation.23 | convolution fusion | flops 271579136 | bytes 5120000 | tf_op jit(solution)/shard_map/cond/branch_1_fun/qhgd,khd->hgqk/dot_general | solution.py:32
  20.9 1.0 fusion.16
  22.0 2.5 %fusion.20 = bf16[4,512,128]{1,2,0:T(8,128)(2,1)S(1)} fusion(f32[4,512]{1,0:T(4,128)S(1)} %broadcast_select_fusion.1, f32[4,512]{1,0:T(4,128)S(1)} %get-tuple-element.118, f32[512,512,4]{1,0,2:T(8,128)S(1)} %get-tuple-element.119, pred[512,512]{0,1:T(8,128)(4,1)S(1)} %fusion.23, bf16[1536,128]{0,1:T(8,128)(2,1)} %copy.52), kind=kOutput, calls=%fused_computation.28 | convolution fusion | flops 274989056 | bytes 5128192 | tf_op jit(solution)/shard_map/cond/branch_1_fun/hgqk,khd->qhgd/dot_general | solution.py:47
  24.5 1.0 copy.68
  25.5 1.1 constant_dynamic-update-slice_fusion.1
  26.6 1.1 constant_dynamic-update-slice_fusion
  27.7 0.7 dynamic-slice_bitcast_fusion.3
  28.4 12.4 %collective-permute-start = (bf16[512,512]{1,0:T(8,128)(2,1)S(1)}, bf16[512,512]{1,0:T(8,128)(2,1)S(1)}, u32[]{:S(2)}, u32[]{:S(2)}) collective-permute-start(bf16[512,512]{1,0:T(8,128)(2,1)S(1)} %dynamic-slice_bitcast_fusion.3), channel_id=1, source_target_pairs={{0,256},{8,264},{16,272},{24,280},{32,288},{40,296},{48,304},{56,3... | collective-permute-start | bytes 1572872 | tf_op jit(solution)/shard_map/ppermute | solution.py:16
  41.3 15.9 %collective-permute-done = bf16[512,512]{1,0:T(8,128)(2,1)S(1)} collective-permute-done((bf16[512,512]{1,0:T(8,128)(2,1)S(1)}, bf16[512,512]{1,0:T(8,128)(2,1)S(1)}, u32[]{:S(2)}, u32[]{:S(2)}) %collective-permute-start) | collective-permute-done | bytes 524320 | tf_op jit(solution)/shard_map/ppermute | solution.py:16
  57.2 0.8 bitcast_dynamic-update-slice_fusion.3
  58.0 0.7 dynamic-slice_bitcast_fusion.2
  58.7 1.9 %collective-permute-start.1 = (bf16[512,512]{1,0:T(8,128)(2,1)S(1)}, bf16[512,512]{1,0:T(8,128)(2,1)S(1)}, u32[]{:S(2)}, u32[]{:S(2)}) collective-permute-start(bf16[512,512]{1,0:T(8,128)(2,1)S(1)} %dynamic-slice_bitcast_fusion.2), channel_id=1, source_target_pairs={{0,128},{8,136},{16,144},{24,152},{32,160},{40,168},{48,176},{56,1... | collective-permute-start | bytes 1572872 | tf_op jit(solution)/shard_map/ppermute | solution.py:16
  61.2 0.7 fusion.50
  61.9 21.7 %collective-permute-done.1 = bf16[512,512]{1,0:T(8,128)(2,1)S(1)} collective-permute-done((bf16[512,512]{1,0:T(8,128)(2,1)S(1)}, bf16[512,512]{1,0:T(8,128)(2,1)S(1)}, u32[]{:S(2)}, u32[]{:S(2)}) %collective-permute-start.1) | collective-permute-done | bytes 524320 | tf_op jit(solution)/shard_map/ppermute | solution.py:16
  83.6 0.8 bitcast_dynamic-update-slice_fusion.2
  84.4 0.7 dynamic-slice_bitcast_fusion.1
  85.2 6.5 %collective-permute-start.2 = (bf16[512,512]{1,0:T(8,128)(2,1)S(1)}, bf16[512,512]{1,0:T(8,128)(2,1)S(1)}, u32[]{:S(2)}, u32[]{:S(2)}) collective-permute-start(bf16[512,512]{1,0:T(8,128)(2,1)S(1)} %dynamic-slice_bitcast_fusion.1), channel_id=1, source_target_pairs={{0,64},{8,72},{16,80},{24,88},{32,96},{40,104},{48,112},{56,120},{... | collective-permute-start | bytes 1572872 | tf_op jit(solution)/shard_map/ppermute | solution.py:16
  92.2 11.5 %collective-permute-done.2 = bf16[512,512]{1,0:T(8,128)(2,1)S(1)} collective-permute-done((bf16[512,512]{1,0:T(8,128)(2,1)S(1)}, bf16[512,512]{1,0:T(8,128)(2,1)S(1)}, u32[]{:S(2)}, u32[]{:S(2)}) %collective-permute-start.2) | collective-permute-done | bytes 524320 | tf_op jit(solution)/shard_map/ppermute | solution.py:16
  103.7 0.8 bitcast_dynamic-update-slice_fusion.1
  104.5 0.7 dynamic-slice_bitcast_fusion
  105.2 1.9 %collective-permute-start.3 = (bf16[512,512]{1,0:T(8,128)(2,1)S(1)}, bf16[512,512]{1,0:T(8,128)(2,1)S(1)}, u32[]{:S(2)}, u32[]{:S(2)}) collective-permute-start(bf16[512,512]{1,0:T(8,128)(2,1)S(1)} %dynamic-slice_bitcast_fusion), channel_id=1, source_target_pairs={{0,32},{8,40},{16,48},{24,56},{32,0},{40,8},{48,16},{56,24},{64,96... | collective-permute-start | bytes 1572872 | tf_op jit(solution)/shard_map/ppermute | solution.py:16
  107.8 14.2 %collective-permute-done.3 = bf16[512,512]{1,0:T(8,128)(2,1)S(1)} collective-permute-done((bf16[512,512]{1,0:T(8,128)(2,1)S(1)}, bf16[512,512]{1,0:T(8,128)(2,1)S(1)}, u32[]{:S(2)}, u32[]{:S(2)}) %collective-permute-start.3) | collective-permute-done | bytes 524320 | tf_op jit(solution)/shard_map/ppermute | solution.py:16
  121.9 0.8 bitcast_dynamic-update-slice_fusion
  122.7 48.8 %all_to_all.19 = bf16[8,192,512]{2,1,0:T(8,128)(2,1)S(1)} all-to-all(bf16[8,192,512]{2,1,0:T(8,128)(2,1)S(1)} %bitcast.151), channel_id=1, replica_groups=mesh['dp'=64,'tensor'=8] {'tensor'}, dimensions={0} | all-to-all | bytes 3145728 | tf_op jit(solution)/shard_map/all_to_all | solution.py:93
  171.5 1.3 copy.71
  (9 shorter events, 0.1 us)
Async XLA Ops:
  0.0 0.7 copy-start
  28.4 28.8 %collective-permute-start = (bf16[512,512]{1,0:T(8,128)(2,1)S(1)}, bf16[512,512]{1,0:T(8,128)(2,1)S(1)}, u32[]{:S(2)}, u32[]{:S(2)}) collective-permute-start(bf16[512,512]{1,0:T(8,128)(2,1)S(1)} %dynamic-slice_bitcast_fusion.3), channel_id=1, source_target_pairs={{0,256},{8,264},{16,272},{24,280},{32,288},{40,296},{48,304},{56,3... | collective-permute-start | bytes 1572872 | tf_op jit(solution)/shard_map/ppermute | solution.py:16
  58.7 24.9 %collective-permute-start.1 = (bf16[512,512]{1,0:T(8,128)(2,1)S(1)}, bf16[512,512]{1,0:T(8,128)(2,1)S(1)}, u32[]{:S(2)}, u32[]{:S(2)}) collective-permute-start(bf16[512,512]{1,0:T(8,128)(2,1)S(1)} %dynamic-slice_bitcast_fusion.2), channel_id=1, source_target_pairs={{0,128},{8,136},{16,144},{24,152},{32,160},{40,168},{48,176},{56,1... | collective-permute-start | bytes 1572872 | tf_op jit(solution)/shard_map/ppermute | solution.py:16
  85.2 18.6 %collective-permute-start.2 = (bf16[512,512]{1,0:T(8,128)(2,1)S(1)}, bf16[512,512]{1,0:T(8,128)(2,1)S(1)}, u32[]{:S(2)}, u32[]{:S(2)}) collective-permute-start(bf16[512,512]{1,0:T(8,128)(2,1)S(1)} %dynamic-slice_bitcast_fusion.1), channel_id=1, source_target_pairs={{0,64},{8,72},{16,80},{24,88},{32,96},{40,104},{48,112},{56,120},{... | collective-permute-start | bytes 1572872 | tf_op jit(solution)/shard_map/ppermute | solution.py:16
  105.2 16.7 %collective-permute-start.3 = (bf16[512,512]{1,0:T(8,128)(2,1)S(1)}, bf16[512,512]{1,0:T(8,128)(2,1)S(1)}, u32[]{:S(2)}, u32[]{:S(2)}) collective-permute-start(bf16[512,512]{1,0:T(8,128)(2,1)S(1)} %dynamic-slice_bitcast_fusion), channel_id=1, source_target_pairs={{0,32},{8,40},{16,48},{24,56},{32,0},{40,8},{48,16},{56,24},{64,96... | collective-permute-start | bytes 1572872 | tf_op jit(solution)/shard_map/ppermute | solution.py:16
where the time goes:
time: 174 us; the launch traced here: 173 us
  waiting for transfers between devices  63.3 us (36%)
  blocking collectives  48.8 us (28%)
  starting transfers between devices  22.7 us (13%)
  local copies, waits for them, and re-layouts  17.8 us (10%)
  other arithmetic  8.07 us (5%)
  matrix products  7.68 us (4%)
  between operations  4.4 us (3%)
    ppermute x4, waiting for transfers between devices, from_partner(): return lax.ppermute(value, axis, pairs)  63.3 us
    all_to_all x1, blocking collectives, local(): lax.all_to_all(attended, 'tensor', split_axis=0, concat_axis=1, tiled=True)  48.8 us
    ppermute x4, starting transfers between devices, from_partner(): return lax.ppermute(value, axis, pairs)  22.7 us
    another operation x4, local copies, waits for them, and re-layouts  6.51 us
    dot_general x2, matrix products, attend_block(): jnp.einsum('hgqk,khd->qhgd', weights, value_three, preferred_element_type...  4.13 us
    dot_general x2, matrix products, attend_block(): jnp.einsum('qhgd,khd->hgqk', query_four, key_three, preferred_element_typ...  3.56 us
  transfers between devices with their start and end apart: 4, of which 4 were waited for; matrix products, arithmetic and copies ran while one was open for 0% of the time, Pallas kernels for 0%

commit v1 on v0

v1 whole, which is shorter than its diff:
```python
import math

import jax
import jax.numpy as jnp
from jax import lax
from jax.experimental import pallas as pl
from jax.experimental.pallas import tpu as pltpu
from jax.sharding import PartitionSpec as P

HEAD_DIM = 128
SECTIONS = 4
BLOCK = 512
TILE = 128
TILES = BLOCK // TILE
BLOCKS = 3
SUBS = 2
GRAIN = 64 // SUBS
GRAINS = BLOCK // GRAIN // SUBS
SCALE = math.log2(math.e) / math.sqrt(HEAD_DIM)
MESH = pl.DeviceIdType.MESH


def kernel(
    heads, shards, levels,
    q_ref, k_ref, v_ref, len_ref, plan_ref, out_ref,
    held, snd, rcv, fin, ids, s_sem, r_sem, as_sem, ar_sem, o_sem,
):
    row = lax.axis_index("dp")
    own = lax.axis_index("tensor")
    chunks = heads * SUBS
    share = BLOCKS * GRAINS // shards

    partners = []
    for section in range(SECTIONS):
        mask = 2 ** (levels - 1 - section)
        partners.append(row + mask * (1 - 2 * ((row // mask) % 2)))
    others = [(own + step) % shards for step in range(1, shards)]

    barrier = pltpu.get_barrier_semaphore()
    for partner in partners:
        pl.semaphore_signal(barrier, inc=1, device_id=(partner, own), device_id_type=MESH)
    for other in others:
        pl.semaphore_signal(barrier, inc=1, device_id=(row, other), device_id_type=MESH)

    endings = []
    total = jnp.int32(0)
    for doc in range(len_ref.shape[0]):
        total = total + len_ref[doc, row]
        endings.append(total)
    for tile in range(BLOCKS * TILES):
        count = jnp.int32(0)
        for ending in endings:
            count = count + jnp.where(ending <= tile * TILE, 1, 0)
        ids[tile] = jnp.where(tile * TILE < total, count, -1)

    lower = lax.broadcasted_iota(jnp.int32, (TILE, TILE), 0) >= lax.broadcasted_iota(
        jnp.int32, (TILE, TILE), 1
    )

    def attend(head):
        columns = slice(head * HEAD_DIM, (head + 1) * HEAD_DIM)

        def block(b, carry):
            start = pl.multiple_of(b * BLOCK, BLOCK)
            for i in range(TILES):
                keys = k_ref[pl.ds(start, (i + 1) * TILE), :]
                scores = lax.dot_general(
                    q_ref[pl.ds(start + i * TILE, TILE), columns], keys,
                    (((1,), (1,)), ((), ())), preferred_element_type=jnp.float32,
                )
                doc = ids[b * TILES + i]
                parts = [
                    scores[:, j * TILE : (j + 1) * TILE]
                    + jnp.where(ids[b * TILES + j] == doc, 0.0, -1e30)
                    for j in range(i)
                ]
                parts.append(jnp.where(lower, scores[:, i * TILE :], -1e30))
                masked = jnp.concatenate(parts, axis=1) if i else parts[0]
                highest = jnp.max(masked, axis=1, keepdims=True)
                powers = jnp.exp2((masked - highest) * SCALE)
                live = jnp.where(doc >= 0, 1.0, 0.0)
                weights = powers * (live / jnp.sum(powers, axis=1, keepdims=True))
                mixed = jnp.dot(
                    weights.astype(jnp.bfloat16), v_ref[pl.ds(start, (i + 1) * TILE), :],
                    preferred_element_type=jnp.float32,
                ).astype(jnp.bfloat16)
                for g in range(TILE // GRAIN):
                    at = i * (TILE // GRAIN) + g
                    held[head * SUBS + at % SUBS, b * GRAINS + at // SUBS] = mixed[
                        g * GRAIN : (g + 1) * GRAIN
                    ]
            return carry

        lax.fori_loop(0, BLOCKS, block, 0)

    def swap_copy(section, c):
        return pltpu.make_async_remote_copy(
            src_ref=snd.at[section, c], dst_ref=rcv.at[section, c],
            send_sem=s_sem.at[section, c], recv_sem=r_sem.at[section, c],
            device_id=(partners[section], own), device_id_type=MESH,
        )

    def share_copy(c, step):
        other = others[step]
        head, sub = c // SUBS, c % SUBS
        column = pl.multiple_of((own * heads + head) * HEAD_DIM, HEAD_DIM)
        return pltpu.make_async_remote_copy(
            src_ref=held.at[c, pl.ds(other * share, share)],
            dst_ref=fin.at[:, sub, :, pl.ds(column, HEAD_DIM)],
            send_sem=as_sem.at[c, step], recv_sem=ar_sem.at[c, step],
            device_id=(row, other), device_id_type=MESH,
        )

    chosen = [plan_ref[section, row] for section in range(SECTIONS)]
    swaps, shares = [], []

    def stage(section, c):
        if section:
            swap_copy(section - 1, c).wait_recv()
            taken = rcv[section - 1, c]
            for b in range(BLOCKS):
                lines = slice(b * GRAINS, (b + 1) * GRAINS)
                held[c, lines] = jnp.where(chosen[section - 1] == b, taken, held[c, lines])
        if section < SECTIONS:
            given = jnp.maximum(chosen[section], 0) * GRAINS
            snd[section, c] = held[c, pl.ds(given, GRAINS)]
            copy = swap_copy(section, c)
            copy.start()
            swaps.append(copy)
        else:
            for step in range(shards - 1):
                copy = share_copy(c, step)
                copy.start()
                shares.append(copy)
            head, sub = c // SUBS, c % SUBS
            column = pl.multiple_of((own * heads + head) * HEAD_DIM, HEAD_DIM)
            fin[:, sub, :, pl.ds(column, HEAD_DIM)] = held[c, pl.ds(own * share, share)]

    for step in range(chunks + SECTIONS):
        if step < chunks and step % SUBS == 0:
            attend(step // SUBS)
        if step == 0:
            pl.semaphore_wait(barrier, SECTIONS + shards - 1)
        for section in range(SECTIONS + 1):
            if 0 <= step - section < chunks:
                stage(section, step - section)

    for copy in swaps:
        copy.wait_send()
    for copy in shares:
        copy.wait()
    done = pltpu.make_async_copy(fin, out_ref, o_sem)
    done.start()
    done.wait()


def solution(mesh):
    ranks, shards = mesh.shape["dp"], mesh.shape["tensor"]
    levels = ranks.bit_length() - 1

    def local(queries, key_rows, values, doc_lengths, swap_plan):
        heads = queries.shape[1] // HEAD_DIM
        chunks = heads * SUBS
        share = BLOCKS * GRAINS // shards
        out_shape = (share, SUBS, GRAIN, shards * heads * HEAD_DIM)
        vmem = pl.BlockSpec(memory_space=pltpu.VMEM)
        smem = pl.BlockSpec(memory_space=pltpu.SMEM)

        def run(*refs):
            kernel(heads, shards, levels, *refs)

        out = pl.pallas_call(
            run,
            out_shape=jax.ShapeDtypeStruct(out_shape, jnp.bfloat16),
            in_specs=[vmem, vmem, vmem, smem, smem],
            out_specs=pl.BlockSpec(memory_space=pl.ANY),
            scratch_shapes=[
                pltpu.VMEM((chunks, BLOCKS * GRAINS, GRAIN, HEAD_DIM), jnp.bfloat16),
                pltpu.VMEM((SECTIONS, chunks, GRAINS, GRAIN, HEAD_DIM), jnp.bfloat16),
                pltpu.VMEM((SECTIONS, chunks, GRAINS, GRAIN, HEAD_DIM), jnp.bfloat16),
                pltpu.VMEM(out_shape, jnp.bfloat16),
                pltpu.SMEM((BLOCKS * TILES,), jnp.int32),
                pltpu.SemaphoreType.DMA((SECTIONS, chunks)),
                pltpu.SemaphoreType.DMA((SECTIONS, chunks)),
                pltpu.SemaphoreType.DMA((chunks, shards - 1)),
                pltpu.SemaphoreType.DMA((chunks, shards - 1)),
                pltpu.SemaphoreType.DMA,
            ],
            compiler_params=pltpu.CompilerParams(
                collective_id=0, has_side_effects=True, vmem_limit_bytes=40 * 2**20
            ),
            name="attend_swap_share",
        )(queries, key_rows, values, doc_lengths.T, swap_plan.T)
        return out.reshape(share * SUBS * GRAIN, shards * heads * HEAD_DIM)

    return jax.shard_map(
        local,
        mesh=mesh,
        in_specs=(P("dp", "tensor"), P("dp", "tensor"), P("dp", "tensor"), P(), P()),
        out_specs=P(("dp", "tensor"), None),
        check_vma=False,
    )
```

time: 174 us -> 91 us (0.52)
  the two profiles are of different devices: /device:TPU:42 before, /device:TPU:8 now
where the time goes in v1:
time: 91 us; the launch traced here: 90.7 us
  Pallas kernels  84.8 us (93%)
  local copies, waits for them, and re-layouts  5.92 us (7%)
    pallas_call x1, Pallas kernels, local(): pl.pallas_call(run, out_shape=jax.ShapeDtypeStruct(out_shape, jnp.bfloat1...  84.8 us
    unnamed x11, local copies, waits for them, and re-layouts  5.92 us

profile of v1, /device:TPU:8, one launch (start us, length us, event | category | flops | bytes accessed | tf_op | source)
XLA Modules:
  0.0 90.7 jit_solution(6641881223601675877)
XLA Ops:
  0.0 0.0 copy-start
  0.0 1.4 %copy-done = bf16[1536,512]{1,0:T(8,128)(2,1)S(1)} copy-done((bf16[1536,512]{1,0:T(8,128)(2,1)S(1)}, bf16[1536,512]{1,0:T(8,128)(2,1)}, u32[]{:S(2)}) %copy-start) | copy-done | bytes 1572888
  1.4 0.0 copy-start.1
  1.4 1.0 %copy-done.1 = bf16[1536,128]{1,0:T(8,128)(2,1)S(1)} copy-done((bf16[1536,128]{1,0:T(8,128)(2,1)S(1)}, bf16[1536,128]{1,0:T(8,128)(2,1)}, u32[]{:S(2)}) %copy-start.1) | copy-done | bytes 393240
  2.4 0.0 copy-start.2
  2.4 1.0 %copy-done.2 = bf16[1536,128]{1,0:T(8,128)(2,1)S(1)} copy-done((bf16[1536,128]{1,0:T(8,128)(2,1)S(1)}, bf16[1536,128]{1,0:T(8,128)(2,1)}, u32[]{:S(2)}) %copy-start.2) | copy-done | bytes 393240
  3.4 0.0 copy-start.3
  3.4 0.7 copy-done.3
  4.1 0.0 copy-start.4
  4.1 0.7 copy-done.4
  4.8 84.8 %attend_swap_share.1 = bf16[3,2,32,4096]{3,2,1,0:T(8,128)(2,1)S(1)} custom-call(bf16[1536,512]{1,0:T(8,128)(2,1)S(1)} %copy-done, bf16[1536,128]{1,0:T(8,128)(2,1)S(1)} %copy-done.1, bf16[1536,128]{1,0:T(8,128)(2,1)S(1)} %copy-done.2, s32[12,64]{1,0:T(8,128)S(1)} %bitcast.4, s32[4,64]{1,0:T(4,128)S(1)} %bitcast.5), custom_call_target="tpu_custom_call" | custom-call | tf_op jit(solution)/shard_map/attend_swap_share/pallas_call | solution.py:172
  89.6 1.1 %copy.7 = bf16[192,4096]{1,0:T(8,128)(2,1)} copy(bf16[192,4096]{1,0:T(8,128)(2,1)S(1)} %bitcast.3) | data formatting | bytes 3145728
Async XLA Ops:
  0.0 1.4 %copy-start = (bf16[1536,512]{1,0:T(8,128)(2,1)S(1)}, bf16[1536,512]{1,0:T(8,128)(2,1)}, u32[]{:S(2)}) copy-start(bf16[1536,512]{1,0:T(8,128)(2,1)} %refs_0_.1) | copy-start | bytes 4718596
  1.4 1.0 %copy-start.1 = (bf16[1536,128]{1,0:T(8,128)(2,1)S(1)}, bf16[1536,128]{1,0:T(8,128)(2,1)}, u32[]{:S(2)}) copy-start(bf16[1536,128]{1,0:T(8,128)(2,1)} %refs_1_.1) | copy-start | bytes 1179652
  2.4 1.0 %copy-start.2 = (bf16[1536,128]{1,0:T(8,128)(2,1)S(1)}, bf16[1536,128]{1,0:T(8,128)(2,1)}, u32[]{:S(2)}) copy-start(bf16[1536,128]{1,0:T(8,128)(2,1)} %refs_2_.1) | copy-start | bytes 1179652
  3.4 0.7 copy-start.3
  4.1 0.7 copy-start.4

commit v2 on v1

v2 whole, which is shorter than its diff:
```python
import math

import jax
import jax.numpy as jnp
from jax import lax
from jax.experimental import pallas as pl
from jax.experimental.pallas import tpu as pltpu
from jax.sharding import PartitionSpec as P

HEAD_DIM = 128
SECTIONS = 4
BLOCK = 512
TILE = 128
TILES = BLOCK // TILE
BLOCKS = 3
SUBS = 4
GRAIN = 64 // SUBS
GRAINS = BLOCK // GRAIN // SUBS
LAGS = (0, 3, 5, 7, 9)
SCALE = math.log2(math.e) / math.sqrt(HEAD_DIM)
MESH = pl.DeviceIdType.MESH


def kernel(
    heads, shards, levels,
    q_hbm, k_hbm, v_hbm, len_hbm, plan_hbm, out_ref,
    q_ref, k_ref, v_ref, len_ref, plan_ref, ids, held, snd, rcv,
    in_sem, s_sem, r_sem, as_sem, ar_sem, o_sem,
):
    row = lax.axis_index("dp")
    own = lax.axis_index("tensor")
    chunks = heads * SUBS
    share = BLOCKS * GRAINS // shards

    partners = []
    for section in range(SECTIONS):
        mask = 2 ** (levels - 1 - section)
        partners.append(row + mask * (1 - 2 * ((row // mask) % 2)))
    others = [(own + step) % shards for step in range(1, shards)]

    barrier = pltpu.get_barrier_semaphore()
    for partner in partners:
        pl.semaphore_signal(barrier, inc=1, device_id=(partner, own), device_id_type=MESH)
    for other in others:
        pl.semaphore_signal(barrier, inc=1, device_id=(row, other), device_id_type=MESH)

    def query_copy(head):
        columns = pl.ds(pl.multiple_of(head * HEAD_DIM, HEAD_DIM), HEAD_DIM)
        return pltpu.make_async_copy(q_hbm.at[:, columns], q_ref.at[head], in_sem.at[head])

    fetches = [
        pltpu.make_async_copy(source, target, in_sem.at[heads + at])
        for at, (source, target) in enumerate(
            [(len_hbm, len_ref), (plan_hbm, plan_ref), (k_hbm, k_ref), (v_hbm, v_ref)]
        )
    ]
    for fetch in fetches[:3] + [query_copy(0)] + fetches[3:]:
        fetch.start()
    for head in range(1, heads):
        query_copy(head).start()

    fetches[0].wait()
    endings = []
    total = jnp.int32(0)
    for doc in range(len_ref.shape[0]):
        total = total + len_ref[doc, row]
        endings.append(total)
    for tile in range(BLOCKS * TILES):
        count = jnp.int32(0)
        for ending in endings:
            count = count + jnp.where(ending <= tile * TILE, 1, 0)
        ids[tile] = jnp.where(tile * TILE < total, count, -1)
    for fetch in fetches[1:]:
        fetch.wait()

    lower = lax.broadcasted_iota(jnp.int32, (TILE, TILE), 0) >= lax.broadcasted_iota(
        jnp.int32, (TILE, TILE), 1
    )

    def attend(head):
        query_copy(head).wait()

        def block(b, carry):
            start = pl.multiple_of(b * BLOCK, BLOCK)
            for i in range(TILES):
                keys = k_ref[pl.ds(start, (i + 1) * TILE), :]
                scores = lax.dot_general(
                    q_ref[head, pl.ds(start + i * TILE, TILE), :], keys,
                    (((1,), (1,)), ((), ())), preferred_element_type=jnp.float32,
                )
                doc = ids[b * TILES + i]
                parts = [
                    scores[:, j * TILE : (j + 1) * TILE]
                    + jnp.where(ids[b * TILES + j] == doc, 0.0, -1e30)
                    for j in range(i)
                ]
                parts.append(jnp.where(lower, scores[:, i * TILE :], -1e30))
                masked = jnp.concatenate(parts, axis=1) if i else parts[0]
                highest = jnp.max(masked, axis=1, keepdims=True)
                powers = jnp.exp2((masked - highest) * SCALE)
                live = jnp.where(doc >= 0, 1.0, 0.0)
                weights = powers * (live / jnp.sum(powers, axis=1, keepdims=True))
                mixed = jnp.dot(
                    weights.astype(jnp.bfloat16), v_ref[pl.ds(start, (i + 1) * TILE), :],
                    preferred_element_type=jnp.float32,
                ).astype(jnp.bfloat16)
                for g in range(TILE // GRAIN):
                    at = i * (TILE // GRAIN) + g
                    held[head * SUBS + at % SUBS, b * GRAINS + at // SUBS] = mixed[
                        g * GRAIN : (g + 1) * GRAIN
                    ]
            return carry

        lax.fori_loop(0, BLOCKS, block, 0)

    def swap_copy(section, c):
        return pltpu.make_async_remote_copy(
            src_ref=snd.at[section, c], dst_ref=rcv.at[section, c],
            send_sem=s_sem.at[section], recv_sem=r_sem.at[section, c],
            device_id=(partners[section], own), device_id_type=MESH,
        )

    def share_copy(c, other):
        head, sub = c // SUBS, c % SUBS
        columns = pl.ds(pl.multiple_of((own * heads + head) * HEAD_DIM, HEAD_DIM), HEAD_DIM)
        return pltpu.make_async_remote_copy(
            src_ref=held.at[c, pl.ds(other * share, share)],
            dst_ref=out_ref.at[:, sub, :, columns],
            send_sem=as_sem, recv_sem=ar_sem,
            device_id=(row, other), device_id_type=MESH,
        )

    def stage(section, c):
        if section:
            swap_copy(section - 1, c).wait_recv()
            taken = rcv[section - 1, c]
            chosen = plan_ref[section - 1, row]
            for b in range(BLOCKS):
                lines = slice(b * GRAINS, (b + 1) * GRAINS)
                held[c, lines] = jnp.where(chosen == b, taken, held[c, lines])
        if section < SECTIONS:
            given = jnp.maximum(plan_ref[section, row], 0) * GRAINS
            snd[section, c] = held[c, pl.ds(given, GRAINS)]
            swap_copy(section, c).start()
        else:
            for other in others:
                share_copy(c, other).start()
            head, sub = c // SUBS, c % SUBS
            columns = pl.ds(pl.multiple_of((own * heads + head) * HEAD_DIM, HEAD_DIM), HEAD_DIM)
            pltpu.make_async_copy(held.at[c, pl.ds(own * share, share)], out_ref.at[:, sub, :, columns], o_sem).start()

    attend(0)
    pl.semaphore_wait(barrier, SECTIONS + shards - 1)

    def step(k, carry):
        @pl.when((k > 0) & (k < chunks) & (k % SUBS == 0))
        def _():
            attend(k // SUBS)

        for section in reversed(range(SECTIONS + 1)):
            c = k - LAGS[section]

            @pl.when((c >= 0) & (c < chunks))
            def _(section=section, c=c):
                stage(section, c)

        return carry

    lax.fori_loop(0, chunks + LAGS[-1], step, 0)

    for section in range(SECTIONS):
        pltpu.make_async_copy(snd.at[section], rcv.at[section], s_sem.at[section]).wait()
    moved = out_ref.at[:, :, :, pl.ds(0, (shards - 1) * heads * HEAD_DIM)]
    pltpu.make_async_copy(moved, moved, as_sem).wait()
    pltpu.make_async_copy(moved, moved, ar_sem).wait()
    kept = out_ref.at[:, :, :, pl.ds(0, heads * HEAD_DIM)]
    pltpu.make_async_copy(kept, kept, o_sem).wait()


def solution(mesh):
    ranks, shards = mesh.shape["dp"], mesh.shape["tensor"]
    levels = ranks.bit_length() - 1

    def local(queries, key_rows, values, doc_lengths, swap_plan):
        tokens, heads = queries.shape[0], queries.shape[1] // HEAD_DIM
        chunks = heads * SUBS
        share = BLOCKS * GRAINS // shards
        out_shape = (share, SUBS, GRAIN, shards * heads * HEAD_DIM)
        lengths, plan = doc_lengths.T, swap_plan.T

        def run(*refs):
            kernel(heads, shards, levels, *refs)

        out = pl.pallas_call(
            run,
            out_shape=pltpu.VMEM(out_shape, jnp.bfloat16),
            in_specs=[pl.BlockSpec(memory_space=pltpu.HBM)] * 5,
            out_specs=pl.BlockSpec(memory_space=pltpu.VMEM),
            scratch_shapes=[
                pltpu.VMEM((heads, tokens, HEAD_DIM), jnp.bfloat16),
                pltpu.VMEM((tokens, HEAD_DIM), jnp.bfloat16),
                pltpu.VMEM((tokens, HEAD_DIM), jnp.bfloat16),
                pltpu.SMEM(lengths.shape, jnp.int32),
                pltpu.SMEM(plan.shape, jnp.int32),
                pltpu.SMEM((BLOCKS * TILES,), jnp.int32),
                pltpu.VMEM((chunks, BLOCKS * GRAINS, GRAIN, HEAD_DIM), jnp.bfloat16),
                pltpu.VMEM((SECTIONS, chunks, GRAINS, GRAIN, HEAD_DIM), jnp.bfloat16),
                pltpu.VMEM((SECTIONS, chunks, GRAINS, GRAIN, HEAD_DIM), jnp.bfloat16),
                pltpu.SemaphoreType.DMA((heads + 4,)),
                pltpu.SemaphoreType.DMA((SECTIONS,)),
                pltpu.SemaphoreType.DMA((SECTIONS, chunks)),
                pltpu.SemaphoreType.DMA,
                pltpu.SemaphoreType.DMA,
                pltpu.SemaphoreType.DMA,
            ],
            compiler_params=pltpu.CompilerParams(
                collective_id=0, has_side_effects=True, vmem_limit_bytes=56 * 2**20
            ),
            name="attend_swap_share",
        )(queries, key_rows, values, lengths, plan)
        return out.reshape(share * SUBS * GRAIN, shards * heads * HEAD_DIM)

    return jax.shard_map(
        local,
        mesh=mesh,
        in_specs=(P("dp", "tensor"), P("dp", "tensor"), P("dp", "tensor"), P(), P()),
        out_specs=P(("dp", "tensor"), None),
        check_vma=False,
    )
```

time: 91 us -> 83 us (0.912)
  local copies, waits for them, and re-layouts: 5.92 us -> 1.15 us
  Pallas kernels: 84.8 us -> 81.7 us
    unnamed x11 -> x1, local copies, waits for them, and re-layouts: 5.92 us -> 1.15 us
    pallas_call x1, Pallas kernels: 84.8 us -> 81.7 us  [local(): pl.pallas_call(run, out_shape=pltpu.VMEM(out_shape, jnp.bfloat16), in_spe...]
where the time goes in v2:
time: 83 us; the launch traced here: 82.9 us
  Pallas kernels  81.7 us (98%)
  local copies, waits for them, and re-layouts  1.15 us (1%)
    pallas_call x1, Pallas kernels, local(): pl.pallas_call(run, out_shape=pltpu.VMEM(out_shape, jnp.bfloat16), in_spe...  81.7 us

profile of v2, /device:TPU:8, one launch (start us, length us, event | category | flops | bytes accessed | tf_op | source)
XLA Modules:
  0.0 82.9 jit_solution(16651959862440253810)
XLA Ops:
  0.0 81.7 %attend_swap_share.1 = bf16[3,4,16,4096]{3,2,1,0:T(8,128)(2,1)S(1)} custom-call(bf16[1536,512]{1,0:T(8,128)(2,1)} %refs_0_.1, bf16[1536,128]{1,0:T(8,128)(2,1)} %refs_1_.1, bf16[1536,128]{1,0:T(8,128)(2,1)} %refs_2_.1, s32[12,64]{1,0:T(8,128)} %bitcast.4, s32[4,64]{1,0:T(4,128)} %bitcast.5), custom_call_target="tpu_custom_call" | custom-call | tf_op jit(solution)/shard_map/attend_swap_share/pallas_call | solution.py:194
  81.7 1.1 %copy.7 = bf16[192,4096]{1,0:T(8,128)(2,1)} copy(bf16[192,4096]{1,0:T(8,128)(2,1)S(1)} %bitcast.3) | data formatting | bytes 3145728

commit v3 on v2

--- a/solution.py
+++ b/solution.py
@@ -16,7 +16,7 @@
 SUBS = 4
 GRAIN = 64 // SUBS
 GRAINS = BLOCK // GRAIN // SUBS
-LAGS = (0, 3, 5, 7, 9)
+LAGS = ((0, 5, 8, 10, 12), (0, 3, 5, 7, 9))
 SCALE = math.log2(math.e) / math.sqrt(HEAD_DIM)
 MESH = pl.DeviceIdType.MESH
 
@@ -149,6 +149,7 @@
             columns = pl.ds(pl.multiple_of((own * heads + head) * HEAD_DIM, HEAD_DIM), HEAD_DIM)
             pltpu.make_async_copy(held.at[c, pl.ds(own * share, share)], out_ref.at[:, sub, :, columns], o_sem).start()
 
+    lags = [even + (odd - even) * (row % 2) for even, odd in zip(*LAGS)]
     attend(0)
     pl.semaphore_wait(barrier, SECTIONS + shards - 1)
 
@@ -158,7 +159,7 @@
             attend(k // SUBS)
 
         for section in reversed(range(SECTIONS + 1)):
-            c = k - LAGS[section]
+            c = k - lags[section]
 
             @pl.when((c >= 0) & (c < chunks))
             def _(section=section, c=c):
@@ -166,7 +167,7 @@
 
         return carry
 
-    lax.fori_loop(0, chunks + LAGS[-1], step, 0)
+    lax.fori_loop(0, chunks + lags[-1], step, 0)
 
     for section in range(SECTIONS):
         pltpu.make_async_copy(snd.at[section], rcv.at[section], s_sem.at[section]).wait()

time: 83 us -> 81.7 us (0.984)
  the two profiles are of different devices: /device:TPU:8 before, /device:TPU:1 now
where the time goes in v3:
time: 81.7 us; the launch traced here: 81.6 us
  Pallas kernels  80.4 us (98%)
  local copies, waits for them, and re-layouts  1.15 us (1%)
    pallas_call x1, Pallas kernels, local(): pl.pallas_call(run, out_shape=pltpu.VMEM(out_shape, jnp.bfloat16), in_spe...  80.4 us

profile of v3, /device:TPU:1, one launch (start us, length us, event | category | flops | bytes accessed | tf_op | source)
XLA Modules:
  0.0 81.6 jit_solution(11569717035762315567)
XLA Ops:
  0.0 80.4 %attend_swap_share.1 = bf16[3,4,16,4096]{3,2,1,0:T(8,128)(2,1)S(1)} custom-call(bf16[1536,512]{1,0:T(8,128)(2,1)} %refs_0_.1, bf16[1536,128]{1,0:T(8,128)(2,1)} %refs_1_.1, bf16[1536,128]{1,0:T(8,128)(2,1)} %refs_2_.1, s32[12,64]{1,0:T(8,128)} %bitcast.4, s32[4,64]{1,0:T(4,128)} %bitcast.5), custom_call_target="tpu_custom_call" | custom-call | tf_op jit(solution)/shard_map/attend_swap_share/pallas_call | solution.py:195
  80.4 1.1 %copy.7 = bf16[192,4096]{1,0:T(8,128)(2,1)} copy(bf16[192,4096]{1,0:T(8,128)(2,1)S(1)} %bitcast.3) | data formatting | bytes 3145728

commit v4 on v3

--- a/solution.py
+++ b/solution.py
@@ -37,11 +37,14 @@
         mask = 2 ** (levels - 1 - section)
         partners.append(row + mask * (1 - 2 * ((row // mask) % 2)))
     others = [(own + step) % shards for step in range(1, shards)]
+    swap_numbers = [partner * shards + own for partner in partners]
+    far_first = sorted(range(1, shards), key=lambda step: -min(step, shards - step))
 
     barrier = pltpu.get_barrier_semaphore()
     for partner in partners:
         pl.semaphore_signal(barrier, inc=1, device_id=(partner, own), device_id_type=MESH)
-    for other in others:
+    for step in far_first:
+        other = (own + step) % shards
         pl.semaphore_signal(barrier, inc=1, device_id=(row, other), device_id_type=MESH)
 
     def query_copy(head):
@@ -117,7 +120,7 @@
         return pltpu.make_async_remote_copy(
             src_ref=snd.at[section, c], dst_ref=rcv.at[section, c],
             send_sem=s_sem.at[section], recv_sem=r_sem.at[section, c],
-            device_id=(partners[section], own), device_id_type=MESH,
+            device_id=swap_numbers[section], device_id_type=pl.DeviceIdType.LOGICAL,
         )
 
     def share_copy(c, other):
@@ -127,7 +130,7 @@
             src_ref=held.at[c, pl.ds(other * share, share)],
             dst_ref=out_ref.at[:, sub, :, columns],
             send_sem=as_sem, recv_sem=ar_sem,
-            device_id=(row, other), device_id_type=MESH,
+            device_id=row * shards + other, device_id_type=pl.DeviceIdType.LOGICAL,
         )
 
     def stage(section, c):

time: 81.7 us -> 81.7 us (level)
  no operation moved by 1% of the time
where the time goes in v4:
time: 81.7 us; the launch traced here: 81.6 us
  Pallas kernels  80.4 us (98%)
  local copies, waits for them, and re-layouts  1.15 us (1%)
    pallas_call x1, Pallas kernels, local(): pl.pallas_call(run, out_shape=pltpu.VMEM(out_shape, jnp.bfloat16), in_spe...  80.4 us

profile of v4, /device:TPU:1, one launch (start us, length us, event | category | flops | bytes accessed | tf_op | source)
XLA Modules:
  0.0 81.6 jit_solution(14805938177316503121)
XLA Ops:
  0.0 80.4 %attend_swap_share.1 = bf16[3,4,16,4096]{3,2,1,0:T(8,128)(2,1)S(1)} custom-call(bf16[1536,512]{1,0:T(8,128)(2,1)} %refs_0_.1, bf16[1536,128]{1,0:T(8,128)(2,1)} %refs_1_.1, bf16[1536,128]{1,0:T(8,128)(2,1)} %refs_2_.1, s32[12,64]{1,0:T(8,128)} %bitcast.4, s32[4,64]{1,0:T(4,128)} %bitcast.5), custom_call_target="tpu_custom_call" | custom-call | tf_op jit(solution)/shard_map/attend_swap_share/pallas_call | solution.py:198
  80.5 1.1 %copy.7 = bf16[192,4096]{1,0:T(8,128)(2,1)} copy(bf16[192,4096]{1,0:T(8,128)(2,1)S(1)} %bitcast.3) | data formatting | bytes 3145728
